TPU v7x, 128 devices: a whole 4x4x4 slice. The times are simulated.
128 devices in a mesh: tm: 4 (over x), mesh: 32 (over y, z, core).
Axes of the slice: x: 4, y: 4, z: 4, core: 2. Of those that a mesh axis runs over, the one named last changes fastest.
Arguments:
- right_sides: bfloat16 [8, 4096, 512], P('tm', 'mesh'), may hold values from -6 to 6
- diag_inverse: bfloat16 [8, 4096, 4096], P('tm', 'mesh'), may hold values from -0.09375 to 0.09375
- coupling: bfloat16 [8, 4096, 4096], P('tm', 'mesh'), may hold values from -0.0625 to 0.0625
- carry_in: bfloat16 [4096, 512], P('mesh'), may hold values from -6 to 6
- arrow_blocks: bfloat16 [8, 64, 4096], P('tm', None, 'mesh'), may hold values from -0.03125 to 0.03125
- tip_right: float32 [64, 512], replicated, may hold values from -6 to 6
- tip_inverse: float32 [64, 64], replicated, may hold values from -0.75 to 0.75
Outputs:
- forward_state: bfloat16 [8, 4096, 512], P('tm', 'mesh')
- tip_solution: float32 [64, 512], replicated
All inputs are finite; a program needn't handle non-finite values.
Results may differ from a plain program's by a relative error of at most 0.011.
Values may be sent and summed in bfloat16 or wider, within the bound.
A program may use at most 64 MiB of HBM per device.

v0:
```python
import jax
import jax.numpy as jnp
from jax import lax
from jax.sharding import PartitionSpec as P


def from_behind(block, axis, distance):
    devices = range(lax.axis_size(axis))
    route = [(i - distance, i) for i in devices if i - distance in devices]
    return lax.ppermute(block, axis, route)


def advance(matrix, source, earlier):
    coupled = jnp.dot(
        matrix,
        lax.all_gather(earlier, "mesh", axis=0, tiled=True),
        preferred_element_type=jnp.float32,
    )
    return (source - coupled).astype(jnp.bfloat16)


def body(right_sides, diag_inverse, coupling, carry_in, arrow_blocks, tip_right, tip_inverse):
    position = lax.axis_index("tm")
    devices_tm = lax.axis_size("tm")
    blocks, own_rows, columns = right_sides.shape
    scaled = jnp.einsum(
        "tij,tjr->tir",
        diag_inverse,
        lax.all_gather(right_sides, "mesh", axis=1, tiled=True),
        preferred_element_type=jnp.float32,
    )
    incoming = carry_in
    outputs = []
    for wave_step in range(devices_tm):
        current = incoming
        outputs = []
        for block_no in range(blocks):
            current = advance(coupling[block_no], scaled[block_no], current)
            outputs.append(current)
        if wave_step + 1 < devices_tm:
            moved = from_behind(current, "tm", 1)
            incoming = jnp.where(position == 0, carry_in, moved)
    solved = jnp.stack(outputs, axis=0)
    arrow_terms = jnp.einsum(
        "tfr,trs->fs", arrow_blocks, solved, preferred_element_type=jnp.float32
    )
    arrow_sum = lax.psum(arrow_terms, ("tm", "mesh"))
    tip_solution = jnp.dot(
        tip_inverse,
        tip_right - arrow_sum,
        precision=lax.Precision.HIGHEST,
        preferred_element_type=jnp.float32,
    )
    return (solved, tip_solution)


def solution(mesh):
    placed = (
        P("tm", "mesh", None),
        P("tm", "mesh", None),
        P("tm", "mesh", None),
        P("mesh", None),
        P("tm", None, "mesh"),
        P(),
        P(),
    )
    return jax.shard_map(
        body, mesh=mesh, in_specs=placed, out_specs=(P("tm", "mesh", None), P()), check_vma=False
    )
```

profile of v0, /device:TPU:1, one launch (start us, length us, event | category | flops | bytes accessed | tf_op | source)
XLA Modules:
  0.0 639.1 jit_solution(520782583988940051)
XLA Ops:
  7.2 0.0 all-gather.10.cloned.1.call-start
  7.2 0.7 all-gather.10.cloned.1.call-update
  7.9 0.0 all-gather.12.cloned.1.call-start
  8.0 0.7 all-gather.12.cloned.1.call-update
  8.7 0.0 all-gather.14.cloned.1.call-start
  8.7 58.4 %all-gather.10.cloned.1.call-done = bf16[2,4096,512]{2,1,0:T(8,128)(2,1)} async-done(((bf16[2,128,512]{2,1,0:T(8,128)(2,1)}), bf16[2,4096,512]{2,1,0:T(8,128)(2,1)}) %all-gather.10.cloned.1.call-update) | async-done | bytes 8388624 | tf_op jit(solution)/shard_map/all_gather | solution.py:29
  67.1 4.6 fusion.33
  71.8 43.6 %all-gather.12.cloned.1.call-done = bf16[4096,512]{1,0:T(8,128)(2,1)} async-done(((bf16[128,512]{1,0:T(8,128)(2,1)}), bf16[4096,512]{1,0:T(8,128)(2,1)}) %all-gather.12.cloned.1.call-update) | async-done | bytes 4194320 | tf_op jit(solution)/shard_map/all_gather | solution.py:16
  115.3 3.9 fusion.7
  119.2 0.0 all-gather.14.cloned.1.call-update
  119.2 0.0 all-gather.16.cloned.1.call-start
  119.3 45.8 %all-gather.14.cloned.1.call-done = bf16[4096,512]{1,0:T(8,128)(2,1)} async-done(((bf16[128,512]{1,0:T(8,128)(2,1)}), bf16[4096,512]{1,0:T(8,128)(2,1)}) %all-gather.14.cloned.1.call-update) | async-done | bytes 4194320 | tf_op jit(solution)/shard_map/all_gather | solution.py:16
  165.1 3.2 fusion.14
  168.3 3.1 collective-permute-start
  171.4 2.6 collective-permute-done
  174.0 0.7 broadcast_select_fusion.2
  174.7 0.0 all-gather.16.cloned.1.call-update
  174.7 0.0 all-gather.18.cloned.1.call-start
  174.8 47.6 %all-gather.16.cloned.1.call-done = bf16[4096,512]{1,0:T(8,128)(2,1)} async-done(((bf16[128,512]{1,0:T(8,128)(2,1)}), bf16[4096,512]{1,0:T(8,128)(2,1)}) %all-gather.16.cloned.1.call-update) | async-done | bytes 4194320 | tf_op jit(solution)/shard_map/all_gather | solution.py:16
  222.4 3.9 fusion.13
  226.3 0.0 all-gather.18.cloned.1.call-update
  226.3 0.0 all-gather.20.cloned.1.call-start
  226.4 45.8 %all-gather.18.cloned.1.call-done = bf16[4096,512]{1,0:T(8,128)(2,1)} async-done(((bf16[128,512]{1,0:T(8,128)(2,1)}), bf16[4096,512]{1,0:T(8,128)(2,1)}) %all-gather.18.cloned.1.call-update) | async-done | bytes 4194320 | tf_op jit(solution)/shard_map/all_gather | solution.py:16
  272.2 3.2 fusion.12
  275.4 3.1 collective-permute-start.1
  278.5 2.6 collective-permute-done.1
  281.1 0.7 broadcast_select_fusion.1
  281.8 0.0 all-gather.20.cloned.1.call-update
  281.8 0.0 all-gather.22.cloned.1.call-start
  281.9 47.6 %all-gather.20.cloned.1.call-done = bf16[4096,512]{1,0:T(8,128)(2,1)} async-done(((bf16[128,512]{1,0:T(8,128)(2,1)}), bf16[4096,512]{1,0:T(8,128)(2,1)}) %all-gather.20.cloned.1.call-update) | async-done | bytes 4194320 | tf_op jit(solution)/shard_map/all_gather | solution.py:16
  329.5 3.9 fusion.11
  333.4 0.0 all-gather.22.cloned.1.call-update
  333.4 0.0 all-gather.24.cloned.1.call-start
  333.4 45.8 %all-gather.22.cloned.1.call-done = bf16[4096,512]{1,0:T(8,128)(2,1)} async-done(((bf16[128,512]{1,0:T(8,128)(2,1)}), bf16[4096,512]{1,0:T(8,128)(2,1)}) %all-gather.22.cloned.1.call-update) | async-done | bytes 4194320 | tf_op jit(solution)/shard_map/all_gather | solution.py:16
  379.2 3.2 fusion.10
  382.5 3.1 collective-permute-start.2
  385.6 2.6 collective-permute-done.2
  388.2 0.7 broadcast_select_fusion
  388.9 0.0 all-gather.26.cloned.1.call-start
  389.0 47.6 %all-gather.24.cloned.1.call-done = bf16[4096,512]{1,0:T(8,128)(2,1)} async-done(((bf16[128,512]{1,0:T(8,128)(2,1)}), bf16[4096,512]{1,0:T(8,128)(2,1)}) %all-gather.24.cloned.1.call-update) | async-done | bytes 4194320 | tf_op jit(solution)/shard_map/all_gather | solution.py:16
  436.6 3.9 fusion.9
  440.5 0.0 all-gather.26.cloned.1.call-update
  440.5 0.0 all-reduce.2.cloned.1.call-start
  440.6 45.8 %all-gather.26.cloned.1.call-done = bf16[4096,512]{1,0:T(8,128)(2,1)} async-done(((bf16[128,512]{1,0:T(8,128)(2,1)}), bf16[4096,512]{1,0:T(8,128)(2,1)}) %all-gather.26.cloned.1.call-update) | async-done | bytes 4194320 | tf_op jit(solution)/shard_map/all_gather | solution.py:16
  486.4 3.2 fusion.15
  489.7 0.8 convolution_bitcast_fusion.7
  490.5 139.9 %all-reduce.2.cloned.1.call-done = f32[64,512]{1,0:T(8,128)} async-done(((f32[64,512]{1,0:T(8,128)}), f32[64,512]{1,0:T(8,128)}) %all-reduce.2.cloned.1.call-update) | async-done | bytes 131088 | tf_op jit(solution)/shard_map/psum | solution.py:47
  630.4 1.8 convolution_bitcast_fusion.8
  (17 shorter events, 0.1 us)
Async XLA Ops:
  7.2 60.0 %copy-start = (bf16[2,128,4096]{2,1,0:T(8,128)(2,1)S(1)}, bf16[2,128,4096]{2,1,0:T(8,128)(2,1)}, u32[]{:S(2)}) copy-start(bf16[2,128,4096]{2,1,0:T(8,128)(2,1)} %param.8) | copy-start | bytes 6291460
  7.2 59.9 %all-gather.10.cloned.1.call-start = ((), (), s32[]{:S(2)}) async-start(), calls=%async_computation | async-start | bytes 8650752 | tf_op jit(solution)/shard_map/all_gather | solution.py:29
  7.9 107.4 %all-gather.12.cloned.1.call-start = ((), (), s32[]{:S(2)}) async-start(), calls=%async_computation.1 | async-start | bytes 4325376 | tf_op jit(solution)/shard_map/all_gather | solution.py:16
  8.7 156.4 %all-gather.14.cloned.1.call-start = ((), (), s32[]{:S(2)}) async-start(), calls=%async_computation.2 | async-start | bytes 4325376 | tf_op jit(solution)/shard_map/all_gather | solution.py:16
  119.2 54.8 %copy-start.1 = (bf16[128,512]{1,0:T(8,128)(2,1)S(1)}, bf16[128,512]{1,0:T(8,128)(2,1)}, u32[]{:S(2)}) copy-start(bf16[128,512]{1,0:T(8,128)(2,1)} %param.10) | copy-start | bytes 393220
  119.2 103.2 %all-gather.16.cloned.1.call-start = ((), (), s32[]{:S(2)}) async-start(), calls=%async_computation.3 | async-start | bytes 4325376 | tf_op jit(solution)/shard_map/all_gather | solution.py:16
  168.3 5.7 collective-permute-start
  174.7 97.4 %all-gather.18.cloned.1.call-start = ((), (), s32[]{:S(2)}) async-start(), calls=%async_computation.4 | async-start | bytes 4325376 | tf_op jit(solution)/shard_map/all_gather | solution.py:16
  226.3 103.2 %all-gather.20.cloned.1.call-start = ((), (), s32[]{:S(2)}) async-start(), calls=%async_computation.5 | async-start | bytes 4325376 | tf_op jit(solution)/shard_map/all_gather | solution.py:16
  275.4 5.7 collective-permute-start.1
  281.8 97.4 %all-gather.22.cloned.1.call-start = ((), (), s32[]{:S(2)}) async-start(), calls=%async_computation.6 | async-start | bytes 4325376 | tf_op jit(solution)/shard_map/all_gather | solution.py:16
  333.4 103.2 %all-gather.24.cloned.1.call-start = ((), (), s32[]{:S(2)}) async-start(), calls=%async_computation.7 | async-start | bytes 4325376 | tf_op jit(solution)/shard_map/all_gather | solution.py:16
  382.5 5.7 collective-permute-start.2
  388.9 97.4 %all-gather.26.cloned.1.call-start = ((), (), s32[]{:S(2)}) async-start(), calls=%async_computation.8 | async-start | bytes 4325376 | tf_op jit(solution)/shard_map/all_gather | solution.py:16
  440.5 49.1 %copy-start.2 = (bf16[128,512]{1,0:T(8,128)(2,1)S(1)}, bf16[128,512]{1,0:T(8,128)(2,1)}, u32[]{:S(2)}) copy-start(bf16[128,512]{1,0:T(8,128)(2,1)} %fusion.9) | copy-start | bytes 393220
  440.5 49.2 %copy-start.5 = (bf16[2,64,128]{2,1,0:T(8,128)(2,1)S(1)}, bf16[2,64,128]{2,1,0:T(8,128)(2,1)}, u32[]{:S(2)}) copy-start(bf16[2,64,128]{2,1,0:T(8,128)(2,1)} %param.11) | copy-start | bytes 98308
  440.5 189.9 %copy-start.4 = (f32[64,512]{1,0:T(8,128)S(1)}, f32[64,512]{1,0:T(8,128)}, u32[]{:S(2)}) copy-start(f32[64,512]{1,0:T(8,128)} %param.12) | copy-start | bytes 393220
  440.5 189.9 %copy-start.6 = (f32[64,64]{1,0:T(8,128)S(1)}, f32[64,64]{1,0:T(8,128)}, u32[]{:S(2)}) copy-start(f32[64,64]{1,0:T(8,128)} %param.13) | copy-start | bytes 49156
  440.5 189.9 %all-reduce.2.cloned.1.call-start = ((), (), s32[]{:S(2)}) async-start(), calls=%async_computation.9 | async-start | bytes 262144 | tf_op jit(solution)/shard_map/psum | solution.py:47
  489.6 142.6 %copy-start.3 = (bf16[2,128,512]{2,1,0:T(8,128)(2,1)}, bf16[2,128,512]{2,1,0:T(8,128)(2,1)S(1)}, u32[]{:S(2)}) copy-start(bf16[2,128,512]{2,1,0:T(8,128)(2,1)S(1)} %pad_maximum_fusion) | copy-start | bytes 786436
Sparse Core Ops, SparseCore 0:
  10.4 56.6 all-gather.9
  69.4 45.8 all-gather.11
  119.4 45.6 all-gather.13
  174.8 47.5 all-gather.15
  226.4 45.6 all-gather.17
  281.9 47.4 all-gather.19
  333.5 45.6 all-gather.21
  389.0 47.5 all-gather.23
  440.6 45.6 all-gather.25
  491.5 138.8 all-reduce.1
where the time goes:
time: 639 us
  waiting for transfers between devices  577 us (90%)
  matrix products  35.8 us (6%)
  between operations  14.3 us (2%)
  starting transfers between devices  9.72 us (2%)
    all_gather x8, waiting for transfers between devices, advance(): lax.all_gather(earlier, 'mesh', axis=0, tiled=True)  370 us
    psum x1, waiting for transfers between devices, body(): arrow_sum = lax.psum(arrow_terms, ('tm', 'mesh'))  140 us
    all_gather x1, waiting for transfers between devices, body(): lax.all_gather(right_sides, 'mesh', axis=1, tiled=True)  58.4 us
    dot_general x8, matrix products, advance(): jnp.dot(matrix, lax.all_gather(earlier, 'mesh', axis=0, tiled=True), pref...  28.5 us
  transfers between devices with their start and end apart: 13, of which 13 were waited for; matrix products, arithmetic and copies ran while one was open for 1% of the time, Pallas kernels for 0%

commit v1 on v0

--- a/solution.py
+++ b/solution.py
@@ -13,7 +13,9 @@
 def advance(matrix, source, earlier):
     coupled = jnp.dot(
         matrix,
-        lax.all_gather(earlier, "mesh", axis=0, tiled=True),
+        jnp.concatenate(
+            lax.all_to_all(jnp.stack([earlier] * lax.axis_size("mesh")), "mesh", 0, 0), axis=0
+        ),
         preferred_element_type=jnp.float32,
     )
     return (source - coupled).astype(jnp.bfloat16)

time: 639 us -> 672 us (1.052)
  blocking collectives: 0 us -> 384 us
  waiting for transfers between devices: 577 us -> 229 us
  matrix products: 35.8 us -> 15.9 us
  starting transfers between devices: 9.72 us -> 21 us
    all_to_all x0 -> x7, blocking collectives: none -> 384 us  [advance(): lax.all_to_all(jnp.stack([earlier] * lax.axis_size('mesh')), 'mesh', 0, 0)]
    all_gather x8 -> x0, waiting for transfers between devices: 370 us -> none  [advance(): lax.all_gather(earlier, 'mesh', axis=0, tiled=True)]
    all_gather x1, waiting for transfers between devices: 58.4 us -> 81.3 us  [body(): lax.all_gather(right_sides, 'mesh', axis=1, tiled=True)]
    dot_general x8, matrix products: 28.5 us -> 8.63 us  [advance(): jnp.dot(matrix, jnp.concatenate(lax.all_to_all(jnp.stack([earlier] * lax....]
    all_to_all x0 -> x1, starting transfers between devices: none -> 9.66 us  [advance(): lax.all_to_all(jnp.stack([earlier] * lax.axis_size('mesh')), 'mesh', 0, 0)]
  transfers between devices with their start and end apart: 13 -> 6, of which waited for: 13 -> 5; matrix products, arithmetic and copies ran while one was open for 1% -> 1% of each run, Pallas kernels for 0% -> 0%
where the time goes in v1:
time: 672 us; the launch traced here: 671 us
  blocking collectives  384 us (57%)
  waiting for transfers between devices  229 us (34%)
  starting transfers between devices  21 us (3%)
  matrix products  15.9 us (2%)
  between operations  14.3 us (2%)
    all_to_all x7, blocking collectives, advance(): lax.all_to_all(jnp.stack([earlier] * lax.axis_size('mesh')), 'mesh', 0, 0)  384 us
    psum x1, waiting for transfers between devices, body(): arrow_sum = lax.psum(arrow_terms, ('tm', 'mesh'))  139 us
    all_gather x1, waiting for transfers between devices, body(): lax.all_gather(right_sides, 'mesh', axis=1, tiled=True)  81.3 us
  transfers between devices with their start and end apart: 6, of which 5 were waited for; matrix products, arithmetic and copies ran while one was open for 1% of the time, Pallas kernels for 0%

profile of v1, /device:TPU:1, one launch (start us, length us, event | category | flops | bytes accessed | tf_op | source)
XLA Modules:
  0.0 671.0 jit_solution(13531949215109856053)
XLA Ops:
  7.2 0.0 copy-start
  7.2 0.0 all-gather.2.cloned.1.call-start
  7.2 0.7 all-gather.2.cloned.1.call-update
  7.9 3.3 stack.22
  11.2 9.7 %all-to-all-start = ((bf16[32,128,512]{2,1,0:T(8,128)(2,1)}), bf16[32,128,512]{2,1,0:T(8,128)(2,1)}, u32[]{:S(2)}, u32[]{:S(2)}) async-start(bf16[32,128,512]{2,1,0:T(8,128)(2,1)} %stack.22), calls=%async_computation | async-start | bytes 8388608 | tf_op jit(solution)/shard_map/all_to_all | solution.py:17
  20.9 0.0 all-reduce.2.cloned.1.call-start
  20.9 81.3 %all-gather.2.cloned.1.call-done = bf16[2,4096,512]{2,1,0:T(8,128)(2,1)} async-done(((bf16[2,128,512]{2,1,0:T(8,128)(2,1)}), bf16[2,4096,512]{2,1,0:T(8,128)(2,1)}) %all-gather.2.cloned.1.call-update) | async-done | bytes 8388624 | tf_op jit(solution)/shard_map/all_gather | solution.py:31
  102.3 0.0 copy-done
  102.3 4.6 fusion.33
  106.9 0.0 all-to-all-done
  106.9 3.2 fusion.7
  110.2 0.5 stack.23
  110.6 0.0 copy-start.2
  110.6 56.0 %all_to_all.40 = bf16[32,128,512]{2,1,0:T(8,128)(2,1)S(1)} all-to-all(bf16[32,128,512]{2,1,0:T(8,128)(2,1)S(1)} %stack.23), channel_id=1, replica_groups=mesh['tm'=4,'mesh'=32] {'mesh'}, dimensions={0} | all-to-all | bytes 8388608 | tf_op jit(solution)/shard_map/all_to_all | solution.py:17
  166.7 0.8 fusion.14
  167.5 3.1 collective-permute-start
  170.6 2.7 collective-permute-done
  173.4 0.5 stack.24
  173.8 54.9 %all_to_all.41 = bf16[32,128,512]{2,1,0:T(8,128)(2,1)S(1)} all-to-all(bf16[32,128,512]{2,1,0:T(8,128)(2,1)S(1)} %stack.24), channel_id=1, replica_groups=mesh['tm'=4,'mesh'=32] {'mesh'}, dimensions={0} | all-to-all | bytes 8388608 | tf_op jit(solution)/shard_map/all_to_all | solution.py:17
  228.7 0.8 fusion.13
  229.5 0.5 stack.25
  230.0 54.4 %all_to_all.42 = bf16[32,128,512]{2,1,0:T(8,128)(2,1)S(1)} all-to-all(bf16[32,128,512]{2,1,0:T(8,128)(2,1)S(1)} %stack.25), channel_id=1, replica_groups=mesh['tm'=4,'mesh'=32] {'mesh'}, dimensions={0} | all-to-all | bytes 8388608 | tf_op jit(solution)/shard_map/all_to_all | solution.py:17
  284.3 0.8 fusion.12
  285.1 4.1 collective-permute-start.1
  289.2 2.7 collective-permute-done.1
  292.0 0.5 stack.26
  292.5 54.9 %all_to_all.43 = bf16[32,128,512]{2,1,0:T(8,128)(2,1)S(1)} all-to-all(bf16[32,128,512]{2,1,0:T(8,128)(2,1)S(1)} %stack.26), channel_id=1, replica_groups=mesh['tm'=4,'mesh'=32] {'mesh'}, dimensions={0} | all-to-all | bytes 8388608 | tf_op jit(solution)/shard_map/all_to_all | solution.py:17
  347.3 0.8 fusion.11
  348.1 0.5 stack.27
  348.6 54.4 %all_to_all.44 = bf16[32,128,512]{2,1,0:T(8,128)(2,1)S(1)} all-to-all(bf16[32,128,512]{2,1,0:T(8,128)(2,1)S(1)} %stack.27), channel_id=1, replica_groups=mesh['tm'=4,'mesh'=32] {'mesh'}, dimensions={0} | all-to-all | bytes 8388608 | tf_op jit(solution)/shard_map/all_to_all | solution.py:17
  403.0 0.8 fusion.10
  403.8 4.1 collective-permute-start.2
  407.9 2.7 collective-permute-done.2
  410.6 0.5 stack.28
  411.1 54.9 %all_to_all.45 = bf16[32,128,512]{2,1,0:T(8,128)(2,1)S(1)} all-to-all(bf16[32,128,512]{2,1,0:T(8,128)(2,1)S(1)} %stack.28), channel_id=1, replica_groups=mesh['tm'=4,'mesh'=32] {'mesh'}, dimensions={0} | all-to-all | bytes 8388608 | tf_op jit(solution)/shard_map/all_to_all | solution.py:17
  466.0 0.8 fusion.9
  466.8 0.5 stack.30
  467.2 0.0 copy-start.3
  467.2 0.0 copy-start.1
  467.3 54.6 %all_to_all.46 = bf16[32,128,512]{2,1,0:T(8,128)(2,1)S(1)} all-to-all(bf16[32,128,512]{2,1,0:T(8,128)(2,1)S(1)} %stack.30), channel_id=1, replica_groups=mesh['tm'=4,'mesh'=32] {'mesh'}, dimensions={0} | all-to-all | bytes 8388608 | tf_op jit(solution)/shard_map/all_to_all | solution.py:17
  521.9 0.7 fusion.15
  522.7 0.0 copy-start.5
  522.7 0.8 convolution_bitcast_fusion.7
  523.5 0.0 all-reduce.2.cloned.1.call-update
  523.5 138.8 %all-reduce.2.cloned.1.call-done = f32[64,512]{1,0:T(8,128)} async-done(((f32[64,512]{1,0:T(8,128)}), f32[64,512]{1,0:T(8,128)}) %all-reduce.2.cloned.1.call-update) | async-done | bytes 131088 | tf_op jit(solution)/shard_map/psum | solution.py:49
  662.3 0.0 copy-done.6
  662.3 1.8 convolution_bitcast_fusion.8
  664.1 0.0 copy-done.1
  (14 shorter events, 0.1 us)
Async XLA Ops:
  7.2 95.1 %copy-start = (bf16[2,128,4096]{2,1,0:T(8,128)(2,1)S(1)}, bf16[2,128,4096]{2,1,0:T(8,128)(2,1)}, u32[]{:S(2)}) copy-start(bf16[2,128,4096]{2,1,0:T(8,128)(2,1)} %param.8) | copy-start | bytes 6291460
  7.2 95.1 %all-gather.2.cloned.1.call-start = ((), (), s32[]{:S(2)}) async-start(), calls=%async_computation.8 | async-start | bytes 8650752 | tf_op jit(solution)/shard_map/all_gather | solution.py:31
  11.2 95.7 %all-to-all-start = ((bf16[32,128,512]{2,1,0:T(8,128)(2,1)}), bf16[32,128,512]{2,1,0:T(8,128)(2,1)}, u32[]{:S(2)}, u32[]{:S(2)}) async-start(bf16[32,128,512]{2,1,0:T(8,128)(2,1)} %stack.22), calls=%async_computation | async-start | bytes 8388608 | tf_op jit(solution)/shard_map/all_to_all | solution.py:17
  20.9 641.4 %all-reduce.2.cloned.1.call-start = ((), (), s32[]{:S(2)}) async-start(), calls=%async_computation.9 | async-start | bytes 262144 | tf_op jit(solution)/shard_map/psum | solution.py:49
  110.6 56.1 %copy-start.2 = (bf16[2,128,4096]{2,1,0:T(8,128)(2,1)S(1)}, bf16[2,128,4096]{2,1,0:T(8,128)(2,1)}, u32[]{:S(2)}) copy-start(bf16[2,128,4096]{2,1,0:T(8,128)(2,1)} %param.9) | copy-start | bytes 6291460
  166.7 6.6 copy-start.4
  167.5 5.9 collective-permute-start
  285.1 6.8 %collective-permute-start.1 = (bf16[128,512]{1,0:T(8,128)(2,1)S(1)}, bf16[128,512]{1,0:T(8,128)(2,1)S(1)}, u32[]{:S(2)}, u32[]{:S(2)}) collective-permute-start(bf16[128,512]{1,0:T(8,128)(2,1)S(1)} %fusion.12), channel_id=1, source_target_pairs={{0,32},{32,64},{64,96},{1,33},{33,65},{65,97},{2,34},{34,66},{66,9... | collective-permute-start | bytes 393224 | tf_op jit(solution)/shard_map/ppermute | solution.py:10
  403.8 6.8 %collective-permute-start.2 = (bf16[128,512]{1,0:T(8,128)(2,1)S(1)}, bf16[128,512]{1,0:T(8,128)(2,1)S(1)}, u32[]{:S(2)}, u32[]{:S(2)}) collective-permute-start(bf16[128,512]{1,0:T(8,128)(2,1)S(1)} %fusion.10), channel_id=1, source_target_pairs={{0,32},{32,64},{64,96},{1,33},{33,65},{65,97},{2,34},{34,66},{66,9... | collective-permute-start | bytes 393224 | tf_op jit(solution)/shard_map/ppermute | solution.py:10
  467.2 54.7 %copy-start.3 = (bf16[2,128,4096]{2,1,0:T(8,128)(2,1)S(1)}, bf16[2,128,4096]{2,1,0:T(8,128)(2,1)}, u32[]{:S(2)}) copy-start(bf16[2,128,4096]{2,1,0:T(8,128)(2,1)} %param.9) | copy-start | bytes 6291460
  467.2 196.9 %copy-start.1 = (bf16[2,128,4096]{2,1,0:T(8,128)(2,1)S(1)}, bf16[2,128,4096]{2,1,0:T(8,128)(2,1)}, u32[]{:S(2)}) copy-start(bf16[2,128,4096]{2,1,0:T(8,128)(2,1)} %param.8) | copy-start | bytes 6291460
  521.9 0.8 copy-start.7
  521.9 140.4 %copy-start.6 = (f32[64,512]{1,0:T(8,128)S(1)}, f32[64,512]{1,0:T(8,128)}, u32[]{:S(2)}) copy-start(f32[64,512]{1,0:T(8,128)} %param.12) | copy-start | bytes 393220
  521.9 140.4 %copy-start.8 = (f32[64,64]{1,0:T(8,128)S(1)}, f32[64,64]{1,0:T(8,128)}, u32[]{:S(2)}) copy-start(f32[64,64]{1,0:T(8,128)} %param.13) | copy-start | bytes 49156
  522.7 141.5 %copy-start.5 = (bf16[2,128,512]{2,1,0:T(8,128)(2,1)}, bf16[2,128,512]{2,1,0:T(8,128)(2,1)S(1)}, u32[]{:S(2)}) copy-start(bf16[2,128,512]{2,1,0:T(8,128)(2,1)S(1)} %pad_maximum_fusion) | copy-start | bytes 786436
Sparse Core Ops, SparseCore 0:
  10.4 91.8 all-gather.1
  523.7 138.5 all-reduce.1
